TPU v7x, 1024 devices: a whole 4x4x32 slice. The times are simulated.
1024 devices in a mesh: ctx: 32 (over y, x, core), tp: 32 (over z).
Axes of the slice: x: 4, y: 4, z: 32, core: 2. Of those that a mesh axis runs over, the one named last changes fastest.
Arguments:
- query: bfloat16 [16384, 4096], P('ctx', 'tp'), may hold values from -6 to 6
- key_proj: bfloat16 [16384, 4096], P('ctx', 'tp'), may hold values from -6 to 6
- value: bfloat16 [16384, 4096], P('ctx', 'tp'), may hold values from -6 to 6
- decay_rates: float32 [16, 4096], P(None, 'tp'), may hold values from 3.0517578e-05 to 0.05
- residues: float32 [16, 4096], P(None, 'tp'), may hold values from -2 to 2
- skip_gain: float32 [4096], P('tp'), may hold values from 0.5 to 1.5
- out_weight: bfloat16 [4096, 4096], P('tp'), may hold values from -0.1875 to 0.1875
Outputs:
- mixed: bfloat16 [16384, 4096], P('ctx', 'tp')
All inputs are finite; a program needn't handle non-finite values.
Results may differ from a plain program's by a relative error of at most 0.006.
Values sent between devices are 32-bit elements; how exact they have to be, the bound alone decides.
No kernel may reach another device: no remote copies, remote signals or barrier semaphores. Data moves between devices by JAX's collectives and lax.ppermute only.
A program may use at most 64 MiB of HBM per device.

v0:
```python
import math

import jax
import jax.numpy as jnp
from jax import lax
from jax.sharding import PartitionSpec as P

highest = lax.Precision.HIGHEST


def angle_table(row_count, col_count, modulus):
    first = lax.broadcasted_iota(jnp.int32, (row_count, col_count), 0)
    second = lax.broadcasted_iota(jnp.int32, (row_count, col_count), 1)
    angles = (first * second % modulus).astype(jnp.float32) * (2.0 * math.pi / modulus)
    return (jnp.cos(angles), jnp.sin(angles))


def first_section(planes, ctx_index, fft_len):
    parts = planes.shape[1]
    offsets = planes.shape[2]
    cos_a, sin_a = angle_table(2 * parts, parts, 2 * parts)
    real_part = jnp.einsum("kp,fpsc->fksc", cos_a, planes, precision=highest)
    imag_part = -jnp.einsum("kp,fpsc->fksc", sin_a, planes, precision=highest)
    coarse = lax.broadcasted_iota(jnp.int32, (2 * parts, offsets), 0)
    offset_ids = ctx_index * offsets + lax.broadcasted_iota(jnp.int32, (2 * parts, offsets), 1)
    angles = (coarse * offset_ids % fft_len).astype(jnp.float32) * (2.0 * math.pi / fft_len)
    cos_t = jnp.cos(angles)[None, :, :, None]
    sin_t = jnp.sin(angles)[None, :, :, None]
    twisted_real = real_part * cos_t + imag_part * sin_t
    twisted_imag = imag_part * cos_t - real_part * sin_t
    return jnp.stack([twisted_real, twisted_imag])


def second_section(spectra):
    length = spectra.shape[3]
    cos_b, sin_b = angle_table(length, length, length)
    real_in = spectra[0]
    imag_in = spectra[1]
    real_out = jnp.einsum("qr,fkrc->fkqc", cos_b, real_in, precision=highest) + jnp.einsum(
        "qr,fkrc->fkqc", sin_b, imag_in, precision=highest
    )
    imag_out = jnp.einsum("qr,fkrc->fkqc", cos_b, imag_in, precision=highest) - jnp.einsum(
        "qr,fkrc->fkqc", sin_b, real_in, precision=highest
    )
    return (real_out, imag_out)


def filter_values(decay_rates, residues, ctx_index, length):
    positions = (ctx_index * length + lax.broadcasted_iota(jnp.int32, (length, 1), 0)).astype(
        jnp.float32
    )
    filter_time = jnp.zeros((length, decay_rates.shape[1]), jnp.float32)
    for mode_id in range(decay_rates.shape[0]):
        rate = decay_rates[mode_id][None, :]
        weight = residues[mode_id][None, :] * jnp.sqrt(-jnp.expm1(-2.0 * rate))
        filter_time = filter_time + weight * jnp.exp(-positions * rate)
    return filter_time


def fourier_conv(signal, decay_rates, residues, ctx_index, parts, length):
    fft_len = 2 * parts * length
    filter_time = filter_values(decay_rates, residues, ctx_index, length)
    moved = (
        lax.all_to_all(signal[None], "ctx", split_axis=1, concat_axis=0, tiled=True),
        lax.all_to_all(filter_time[None], "ctx", split_axis=1, concat_axis=0, tiled=True),
    )
    sectioned = first_section(jnp.stack([moved[0], moved[1]]), ctx_index, fft_len)
    spectra = lax.all_to_all(sectioned, "ctx", split_axis=2, concat_axis=3, tiled=True)
    real_out, imag_out = second_section(spectra)
    sig_real, sig_imag = (real_out[0], imag_out[0])
    fil_real, fil_imag = (real_out[1], imag_out[1])
    prod_real = sig_real * fil_real - sig_imag * fil_imag
    prod_imag = sig_real * fil_imag + sig_imag * fil_real
    cos_b, sin_b = angle_table(length, length, length)
    back_real = jnp.einsum("rq,kqc->krc", cos_b, prod_real, precision=highest) - jnp.einsum(
        "rq,kqc->krc", sin_b, prod_imag, precision=highest
    )
    back_imag = jnp.einsum("rq,kqc->krc", cos_b, prod_imag, precision=highest) + jnp.einsum(
        "rq,kqc->krc", sin_b, prod_real, precision=highest
    )
    coarse = 2 * ctx_index + lax.broadcasted_iota(jnp.int32, (2, length), 0)
    offset_ids = lax.broadcasted_iota(jnp.int32, (2, length), 1)
    angles = (coarse * offset_ids % fft_len).astype(jnp.float32) * (2.0 * math.pi / fft_len)
    cos_t = jnp.cos(angles)[:, :, None]
    sin_t = jnp.sin(angles)[:, :, None]
    twisted_real = back_real * cos_t - back_imag * sin_t
    twisted_imag = back_imag * cos_t + back_real * sin_t
    regrouped = lax.all_to_all(
        jnp.stack([twisted_real, twisted_imag]), "ctx", split_axis=2, concat_axis=1, tiled=True
    )
    cos_d, sin_d = angle_table(parts, 2 * parts, 2 * parts)
    blocks = (
        jnp.einsum("pk,ksc->psc", cos_d, regrouped[0], precision=highest)
        - jnp.einsum("pk,ksc->psc", sin_d, regrouped[1], precision=highest)
    ) * (1.0 / fft_len)
    joined = lax.all_to_all(blocks, "ctx", split_axis=0, concat_axis=1, tiled=True)
    return joined[0]


def per_device(query, key_proj, value, decay_rates, residues, skip_gain, out_weight):
    parts = lax.axis_size("ctx")
    ctx_index = lax.axis_index("ctx")
    length = query.shape[0]
    signal = key_proj.astype(jnp.float32) * value.astype(jnp.float32)
    conv = fourier_conv(signal, decay_rates, residues, ctx_index, parts, length)
    gated = (query.astype(jnp.float32) * (conv + skip_gain[None, :] * signal)).astype(jnp.bfloat16)
    summed = lax.psum_scatter(
        lax.dot_general(
            out_weight, gated, (((0,), (1,)), ((), ())), preferred_element_type=jnp.float32
        ),
        "tp",
        scatter_dimension=0,
        tiled=True,
    )
    return summed.T.astype(jnp.bfloat16)


def solution(mesh):
    placed = (
        P("ctx", "tp"),
        P("ctx", "tp"),
        P("ctx", "tp"),
        P(None, "tp"),
        P(None, "tp"),
        P("tp"),
        P("tp", None),
    )
    return jax.shard_map(
        per_device, mesh=mesh, in_specs=placed, out_specs=P("ctx", "tp"), check_vma=False
    )
```

profile of v0, /device:TPU:6, one launch (start us, length us, event | category | flops | bytes accessed | tf_op | source)
XLA Modules:
  0.0 337.6 jit_solution(15200853441194716749)
XLA Ops:
  6.5 1.8 convert_multiply_fusion
  8.3 16.7 %all-to-all-start = ((f32[1,512,128]{2,0,1:T(1,128)}), f32[1,512,128]{2,0,1:T(1,128)S(1)}, u32[]{:S(2)}, u32[]{:S(2)}) async-start(f32[1,512,128]{2,0,1:T(1,128)} %bitcast.2), calls=%async_computation | async-start | bytes 524288 | tf_op jit(solution)/shard_map/all_to_all | solution.py:64
  25.0 1.0 slice_bitcast_fusion.9
  26.0 1.0 multiply_bitcast_fusion.15
  27.0 1.0 multiply_bitcast_fusion.14
  28.0 1.5 multiply_add_fusion.1
  29.5 2.6 all-to-all-done
  32.1 5.7 %all-to-all-start.1 = ((f32[1,512,128]{2,0,1:T(1,128)}), f32[1,512,128]{2,0,1:T(1,128)S(1)}, u32[]{:S(2)}, u32[]{:S(2)}) async-start(f32[1,512,128]{2,0,1:T(1,128)} %bitcast.36), calls=%async_computation.1 | async-start | bytes 524288 | tf_op jit(solution)/shard_map/all_to_all | solution.py:65
  37.8 0.1 fusion.73
  37.9 0.1 copy_dynamic-update-slice_fusion.1
  38.0 6.9 %all-to-all-done.1 = f32[1,512,128]{2,0,1:T(1,128)S(1)} async-done(((f32[1,512,128]{2,0,1:T(1,128)}), f32[1,512,128]{2,0,1:T(1,128)S(1)}, u32[]{:S(2)}, u32[]{:S(2)}) %all-to-all-start.1) | async-done | bytes 262176 | tf_op jit(solution)/shard_map/all_to_all | solution.py:65
  44.9 0.1 copy_dynamic-update-slice_fusion
  45.0 1.1 fusion
  46.1 1.5 add_bitcast_fusion
  47.6 0.2 pad_maximum_fusion
  47.8 2.6 copy.56
  50.4 5.8 %all-to-all-start.2 = ((f32[2,2,64,16,128]{4,3,1,0,2:T(8,128)}), f32[2,2,64,16,128]{4,3,1,0,2:T(8,128)S(1)}, u32[]{:S(2)}, u32[]{:S(2)}) async-start(f32[2,2,64,16,128]{4,3,1,0,2:T(8,128)} %copy.56), calls=%async_computation.2 | async-start | bytes 4194304 | tf_op jit(solution)/shard_map/all_to_all | solution.py:68
  56.2 0.0 reduce-scatter.2.cloned.1.call-start
  56.3 0.2 fusion.75
  56.4 25.4 %all-to-all-done.2 = f32[2,2,64,16,128]{4,3,1,0,2:T(8,128)S(1)} async-done(((f32[2,2,64,16,128]{4,3,1,0,2:T(8,128)}), f32[2,2,64,16,128]{4,3,1,0,2:T(8,128)S(1)}, u32[]{:S(2)}, u32[]{:S(2)}) %all-to-all-start.2) | async-done | bytes 2097184 | tf_op jit(solution)/shard_map/all_to_all | solution.py:68
  81.8 0.2 copy.57
  82.0 0.2 fusion.124
  82.2 0.1 copy.58
  82.3 8.0 %fusion.17 = f32[2,2,128,512]{3,2,1,0:T(8,128)S(1)} fusion(f32[2,2,512,128]{3,2,1,0:T(8,128)S(1)} %bitcast.182), kind=kOutput, calls=%fused_computation.30 | convolution fusion | flops 1614282752 | bytes 2097152 | tf_op jit(solution)/shard_map/qr,fkrc->fkqc/dot_general | solution.py:39
  90.3 0.1 copy.60
  90.3 7.5 %fusion.15 = f32[2,2,128,512]{3,2,1,0:T(8,128)S(1)} fusion(f32[2,2,512,128]{3,2,1,0:T(8,128)S(1)} %bitcast.184), kind=kOutput, calls=%fused_computation.28 | convolution fusion | flops 1614282752 | bytes 2097152 | tf_op jit(solution)/shard_map/qr,fkrc->fkqc/dot_general | solution.py:42
  97.9 7.6 %fusion.2 = f32[2,2,512,128]{2,3,1,0:T(8,128)S(1)} fusion(f32[2,2,128,512]{3,2,1,0:T(8,128)S(1)} %fusion.17, f32[2,2,512,128]{3,2,1,0:T(8,128)S(1)} %bitcast.185), kind=kOutput, calls=%fused_computation.11 | convolution fusion | flops 1614544896 | bytes 3145728 | tf_op jit(solution)/shard_map/qr,fkrc->fkqc/dot_general | solution.py:39
  105.4 7.7 %fusion.1 = f32[2,2,512,128]{2,3,1,0:T(8,128)S(1)} fusion(f32[2,2,128,512]{3,2,1,0:T(8,128)S(1)} %fusion.15, f32[2,2,512,128]{3,2,1,0:T(8,128)S(1)} %bitcast.183), kind=kOutput, calls=%fused_computation.9 | convolution fusion | flops 1614544896 | bytes 3145728 | tf_op jit(solution)/shard_map/qr,fkrc->fkqc/dot_general | solution.py:42
  113.2 0.2 multiply_add_fusion
  113.4 5.3 %fusion.9 = f32[2,128,512]{2,1,0:T(8,128)S(1)} fusion(f32[1,2,512,128]{2,3,1,0:T(8,128)S(1)} %get-tuple-element.7), kind=kOutput, calls=%fused_computation.22 | convolution fusion | flops 808976384 | bytes 1048576 | tf_op jit(solution)/shard_map/rq,kqc->krc/dot_general | solution.py:78
  118.8 5.3 %fusion.11 = f32[2,128,512]{2,1,0:T(8,128)S(1)} fusion(f32[1,2,512,128]{2,3,1,0:T(8,128)S(1)} %get-tuple-element.8), kind=kOutput, calls=%fused_computation.24 | convolution fusion | flops 808976384 | bytes 1048576 | tf_op jit(solution)/shard_map/rq,kqc->krc/dot_general | solution.py:75
  124.1 5.5 %convolution_add_fusion.1 = f32[2,128,512]{2,1,0:T(8,128)S(1)} fusion(f32[2,128,512]{2,1,0:T(8,128)S(1)} %fusion.9, f32[1,2,512,128]{2,3,1,0:T(8,128)S(1)} %get-tuple-element.8), kind=kOutput, calls=%fused_computation.12 | convolution fusion | flops 809107456 | bytes 1572864 | tf_op jit(solution)/shard_map/rq,kqc->krc/dot_general | solution.py:78
  129.6 5.4 %subtract_bitcast_fusion.1 = (f32[1,2,512,128]{2,3,1,0:T(8,128)S(1)}, f32[1,2,512,128]{2,3,1,0:T(8,128)S(1)}) fusion(f32[2,128,512]{2,1,0:T(8,128)S(1)} %convolution_add_fusion.1, f32[2,512]{1,0:T(2,128)S(1)} %get-tuple-element.48, f32[2,512]{1,0:T(2,128)S(1)} %get-tuple-element.47, f32[2,128,512]{2,1,0:T(8,128)S(1)} %fusion.11, ...), kind=kOutput, calls=%fused_computation.42 | convolution fusion | flops 809893888 | bytes 2629632 | tf_op jit(solution)/shard_map/rq,kqc->krc/dot_general | solution.py:75
  135.1 0.1 pad_maximum_fusion.1
  135.1 0.7 copy.64
  135.9 22.1 %all_to_all.63 = f32[2,2,512,128]{3,1,0,2:T(2,128)S(1)} all-to-all(f32[2,2,512,128]{3,1,0,2:T(2,128)S(1)} %copy.64), channel_id=1, replica_groups=mesh['ctx'=32,'tp'=32] {'ctx'}, dimensions={2} | all-to-all | bytes 2097152 | tf_op jit(solution)/shard_map/all_to_all | solution.py:88
  158.0 0.1 copy.65
  158.0 0.1 fusion.125
  158.1 0.4 copy.67
  158.6 0.4 copy.66
  159.0 0.5 fusion.47
  159.5 0.5 fusion.3
  159.9 0.2 copy.68
  160.1 13.0 %all_to_all.64 = f32[32,16,128]{2,1,0:T(8,128)S(1)} all-to-all(f32[32,16,128]{2,1,0:T(8,128)S(1)} %copy.68), channel_id=1, replica_groups=mesh['ctx'=32,'tp'=32] {'ctx'}, dimensions={0} | all-to-all | bytes 524288 | tf_op jit(solution)/shard_map/all_to_all | solution.py:96
  173.1 0.1 fusion.37
  173.2 4.5 %convolution_bitcast_fusion = f32[4096,512]{0,1:T(8,128)} fusion(bf16[512,128]{1,0:T(8,128)(2,1)S(1)} %fusion.37, bf16[128,4096]{1,0:T(8,128)(2,1)S(1)} %copy-done), kind=kOutput, calls=%fused_computation | convolution fusion | flops 536870912 | bytes 9568256 | tf_op jit(solution)/shard_map/dot_general | solution.py:108
  177.7 151.2 %reduce-scatter.2.cloned.1.call-done = f32[128,512]{0,1:T(8,128)} async-done(((f32[4096,512]{0,1:T(8,128)}), f32[128,512]{0,1:T(8,128)}) %reduce-scatter.2.cloned.1.call-update) | async-done | bytes 262160 | tf_op jit(solution)/shard_map/reduce_scatter | solution.py:107
  328.9 1.6 convert_bitcast_fusion
  (14 shorter events, 0.1 us)
Async XLA Ops:
  6.5 166.7 %copy-start = (bf16[128,4096]{1,0:T(8,128)(2,1)S(1)}, bf16[128,4096]{1,0:T(8,128)(2,1)}, u32[]{:S(2)}) copy-start(bf16[128,4096]{1,0:T(8,128)(2,1)} %param.13) | copy-start | bytes 3145732
  8.3 23.8 %all-to-all-start = ((f32[1,512,128]{2,0,1:T(1,128)}), f32[1,512,128]{2,0,1:T(1,128)S(1)}, u32[]{:S(2)}, u32[]{:S(2)}) async-start(f32[1,512,128]{2,0,1:T(1,128)} %bitcast.2), calls=%async_computation | async-start | bytes 524288 | tf_op jit(solution)/shard_map/all_to_all | solution.py:64
  32.1 12.8 %all-to-all-start.1 = ((f32[1,512,128]{2,0,1:T(1,128)}), f32[1,512,128]{2,0,1:T(1,128)S(1)}, u32[]{:S(2)}, u32[]{:S(2)}) async-start(f32[1,512,128]{2,0,1:T(1,128)} %bitcast.36), calls=%async_computation.1 | async-start | bytes 524288 | tf_op jit(solution)/shard_map/all_to_all | solution.py:65
  50.4 31.5 %all-to-all-start.2 = ((f32[2,2,64,16,128]{4,3,1,0,2:T(8,128)}), f32[2,2,64,16,128]{4,3,1,0,2:T(8,128)S(1)}, u32[]{:S(2)}, u32[]{:S(2)}) async-start(f32[2,2,64,16,128]{4,3,1,0,2:T(8,128)} %copy.56), calls=%async_computation.2 | async-start | bytes 4194304 | tf_op jit(solution)/shard_map/all_to_all | solution.py:68
  56.2 272.7 %reduce-scatter.2.cloned.1.call-start = ((), (), s32[]{:S(2)}) async-start(), calls=%async_computation.6 | async-start | bytes 8650752 | tf_op jit(solution)/shard_map/reduce_scatter | solution.py:107
  158.5 14.6 %copy-start.1 = (bf16[512,128]{1,0:T(8,128)(2,1)S(1)}, bf16[512,128]{1,0:T(8,128)(2,1)}, u32[]{:S(2)}) copy-start(bf16[512,128]{1,0:T(8,128)(2,1)} %param.9) | copy-start | bytes 393220
  158.5 14.6 %copy-start.2 = (bf16[512,128]{1,0:T(8,128)(2,1)S(1)}, bf16[512,128]{1,0:T(8,128)(2,1)}, u32[]{:S(2)}) copy-start(bf16[512,128]{1,0:T(8,128)(2,1)} %param.8) | copy-start | bytes 393220
  158.6 14.6 %copy-start.3 = (bf16[512,128]{1,0:T(8,128)(2,1)S(1)}, bf16[512,128]{1,0:T(8,128)(2,1)}, u32[]{:S(2)}) copy-start(bf16[512,128]{1,0:T(8,128)(2,1)} %param.7) | copy-start | bytes 393220
  158.6 14.6 %copy-start.4 = (f32[128]{0:T(128)S(1)}, f32[128]{0:T(128)}, u32[]{:S(2)}) copy-start(f32[128]{0:T(128)} %param.12) | copy-start | bytes 1540
Sparse Core Ops, SparseCore 0:
  177.9 151.0 reduce-scatter.1
where the time goes:
time: 344 us; the launch traced here: 338 us
  waiting for transfers between devices  186 us (54%)
  matrix products  60.4 us (18%)
  blocking collectives  35.1 us (10%)
  starting transfers between devices  28.2 us (8%)
  between operations  14 us (4%)
  other arithmetic  7.73 us (2%)
  local copies, waits for them, and re-layouts  6.1 us (2%)
    reduce_scatter x1, waiting for transfers between devices, per_device(): lax.psum_scatter(lax.dot_general(out_weight, gated, (((0,), (1,)), ((), (...  151 us
    all_to_all x1, waiting for transfers between devices, fourier_conv(): lax.all_to_all(sectioned, 'ctx', split_axis=2, concat_axis=3, tiled=True)  25.4 us
    all_to_all x1, blocking collectives, fourier_conv(): lax.all_to_all(jnp.stack([twisted_real, twisted_imag]), 'ctx', split_axis...  22.1 us
    all_to_all x1, starting transfers between devices, fourier_conv(): lax.all_to_all(signal[None], 'ctx', split_axis=1, concat_axis=0, tiled=True)  16.7 us
    all_to_all x1, blocking collectives, fourier_conv(): lax.all_to_all(blocks, 'ctx', split_axis=0, concat_axis=1, tiled=True)  13 us
    dot_general x1, matrix products, second_section(): jnp.einsum('qr,fkrc->fkqc', cos_b, real_in, precision=highest)  7.98 us
    dot_general x1, matrix products, second_section(): jnp.einsum('qr,fkrc->fkqc', sin_b, real_in, precision=highest)  7.74 us
    dot_general x1, matrix products, second_section(): jnp.einsum('qr,fkrc->fkqc', sin_b, imag_in, precision=highest)  7.57 us
  transfers between devices with their start and end apart: 4, of which 4 were waited for; matrix products, arithmetic and copies ran while one was open for 1% of the time, Pallas kernels for 0%

commit v1 on v0

v1 whole, which is shorter than its diff:
```python
import functools

import jax
import jax.numpy as jnp
from jax import lax
from jax.experimental import pallas as pl
from jax.experimental.pallas import tpu as pltpu
from jax.sharding import PartitionSpec as P

chunks = 8


def mode_rows(values, mode_count):
    return [jnp.broadcast_to(values[m : m + 1, :], (chunks, values.shape[1])) for m in range(mode_count)]


def states_kernel(key_ref, value_ref, rate_ref, chunk_ref, end_ref, signal_ref):
    modes = rate_ref.shape[0]
    steps = key_ref.shape[0] // chunks
    signal_ref[...] = key_ref[...].astype(jnp.float32) * value_ref[...].astype(jnp.float32)
    rates = rate_ref[...]
    decays = mode_rows(jnp.exp(-rates), modes)

    def step(t, states):
        x = signal_ref[pl.ds(t, chunks, stride=steps), :]
        return tuple(decays[m] * states[m] + x for m in range(modes))

    zero = jnp.zeros((chunks, rates.shape[1]), jnp.float32)
    states = lax.fori_loop(0, steps, step, (zero,) * modes, unroll=8)
    for m in range(modes):
        chunk_ref[pl.ds(m, chunks, stride=modes), :] = states[m]
    chunk_decay = jnp.exp(-float(steps) * rates)
    end = jnp.zeros_like(rates)
    for c in range(chunks):
        end = chunk_decay * end + chunk_ref[c * modes : (c + 1) * modes, :]
    end_ref[...] = end


def gated_kernel(
    index_ref, ends_ref, chunk_ref, rate_ref, weight_ref, skip_ref, query_ref, signal_ref, gated_ref, start_ref, wide_ref
):
    modes = rate_ref.shape[0]
    length = query_ref.shape[0]
    steps = length // chunks
    index = index_ref[0]
    rates = rate_ref[...]
    block_decay = jnp.exp(-float(length) * rates)
    carry = jnp.zeros_like(rates)
    for d in range(ends_ref.shape[0]):
        carry = jnp.where(d < index, block_decay * carry + ends_ref[d], carry)
    chunk_decay = jnp.exp(-float(steps) * rates)
    for c in range(chunks):
        rows = slice(c * modes, (c + 1) * modes)
        start_ref[rows, :] = carry
        carry = chunk_decay * carry + chunk_ref[rows, :]
    decays = mode_rows(jnp.exp(-rates), modes)
    weights = mode_rows(weight_ref[...], modes)
    skip = jnp.broadcast_to(skip_ref[...], (chunks, rates.shape[1]))
    wide_ref[...] = query_ref[...].astype(jnp.float32)

    def step(t, states):
        rows = pl.ds(t, chunks, stride=steps)
        x = signal_ref[rows, :]
        after = tuple(decays[m] * states[m] + x for m in range(modes))
        terms = [weights[m] * after[m] for m in range(modes)]
        while len(terms) > 1:
            terms = [terms[i] + terms[i + 1] for i in range(0, len(terms), 2)]
        wide_ref[rows, :] = wide_ref[rows, :] * (terms[0] + skip * x)
        return after

    states = tuple(start_ref[pl.ds(m, chunks, stride=modes), :] for m in range(modes))
    lax.fori_loop(0, steps, step, states, unroll=4)
    gated_ref[...] = wide_ref[...].astype(jnp.bfloat16)


def gated_block(query, key_proj, value, decay_rates, residues, skip_gain):
    length, width = query.shape
    modes = decay_rates.shape[0]
    shape = functools.partial(jax.ShapeDtypeStruct, dtype=jnp.float32)
    chunk_states, end_state, signal = pl.pallas_call(
        states_kernel,
        out_shape=(shape((chunks * modes, width)), shape((modes, width)), shape((length, width))),
    )(key_proj, value, decay_rates)
    ends = lax.all_gather(end_state, "ctx")
    weights = residues * jnp.sqrt(-jnp.expm1(-2.0 * decay_rates))
    vmem = pl.BlockSpec(memory_space=pltpu.VMEM)
    return pl.pallas_call(
        gated_kernel,
        out_shape=jax.ShapeDtypeStruct((length, width), jnp.bfloat16),
        in_specs=[pl.BlockSpec(memory_space=pltpu.SMEM)] + [vmem] * 7,
        out_specs=vmem,
        scratch_shapes=[pltpu.VMEM((chunks * modes, width), jnp.float32), pltpu.VMEM((length, width), jnp.float32)],
    )(lax.axis_index("ctx").reshape(1), ends, chunk_states, decay_rates, weights, skip_gain[None, :], query, signal)


def per_device(query, key_proj, value, decay_rates, residues, skip_gain, out_weight):
    gated = gated_block(query, key_proj, value, decay_rates, residues, skip_gain)
    summed = lax.psum_scatter(
        lax.dot_general(
            out_weight, gated, (((0,), (1,)), ((), ())), preferred_element_type=jnp.float32
        ),
        "tp",
        scatter_dimension=0,
        tiled=True,
    )
    return summed.T.astype(jnp.bfloat16)


def solution(mesh):
    placed = (
        P("ctx", "tp"),
        P("ctx", "tp"),
        P("ctx", "tp"),
        P(None, "tp"),
        P(None, "tp"),
        P("tp"),
        P("tp", None),
    )
    return jax.shard_map(
        per_device, mesh=mesh, in_specs=placed, out_specs=P("ctx", "tp"), check_vma=False
    )
```

time: 344 us -> 214 us (0.62); the launches traced: 338 us -> 214 us
  matrix products: 60.4 us -> 5.37 us
  waiting for transfers between devices: 186 us -> 150 us
  starting transfers between devices: 28.2 us -> 0.01 us
  local copies, waits for them, and re-layouts: 6.1 us -> 0.01 us
  Pallas kernels: 0 us -> 5.12 us
  other arithmetic: 7.73 us -> 3.04 us
    dot_general x12 -> x0, matrix products: 55.9 us -> none  [the longest x1 7.98 us: second_section(): jnp.einsum('qr,fkrc->fkqc', cos_b, real_in, precision=highest)]
    all_gather x0 -> x1, blocking collectives: none -> 36.8 us  [gated_block(): ends = lax.all_gather(end_state, 'ctx')]
    all_to_all x2 -> x0, blocking collectives: 35.1 us -> none  [the longest x1 22.1 us: fourier_conv(): lax.all_to_all(jnp.stack([twisted_real, twisted_imag]), 'ctx', split_axis...]
    all_to_all x3 -> x0, waiting for transfers between devices: 34.9 us -> none  [the longest x1 25.4 us: fourier_conv(): lax.all_to_all(sectioned, 'ctx', split_axis=2, concat_axis=3, tiled=True)]
    all_to_all x3 -> x0, starting transfers between devices: 28.2 us -> none  [the longest x1 16.7 us: fourier_conv(): lax.all_to_all(signal[None], 'ctx', split_axis=1, concat_axis=0, tiled=True)]
    pallas_call x0 -> x2, Pallas kernels: none -> 5.12 us  [the longest x1 2.99 us: gated_block(): pl.pallas_call(gated_kernel, out_shape=jax.ShapeDtypeStruct((length, widt...]
  transfers between devices with their start and end apart: 4 -> 1, of which waited for: 4 -> 1; matrix products, arithmetic and copies ran while one was open for 1% -> 0% of each run, Pallas kernels for 0% -> 0%
where the time goes in v1:
time: 214 us
  waiting for transfers between devices  150 us (70%)
  blocking collectives  36.8 us (17%)
  between operations  13.4 us (6%)
  matrix products  5.37 us (3%)
  Pallas kernels  5.12 us (2%)
  other arithmetic  3.04 us (1%)
    reduce_scatter x1, waiting for transfers between devices, per_device(): lax.psum_scatter(lax.dot_general(out_weight, gated, (((0,), (1,)), ((), (...  150 us
    all_gather x1, blocking collectives, gated_block(): ends = lax.all_gather(end_state, 'ctx')  36.8 us
    dot_general x1, matrix products, per_device(): lax.dot_general(out_weight, gated, (((0,), (1,)), ((), ())), preferred_el...  5.37 us
  transfers between devices with their start and end apart: 1, of which 1 were waited for; matrix products, arithmetic and copies ran while one was open for 0% of the time, Pallas kernels for 0%

profile of v1, /device:TPU:6, one launch (start us, length us, event | category | flops | bytes accessed | tf_op | source)
XLA Modules:
  0.0 214.1 jit_solution(3948388664912465856)
XLA Ops:
  6.5 0.0 copy-start
  6.5 0.0 reduce-scatter.2.cloned.1.call-start
  6.5 1.4 sqrt_multiply_fusion.weight_ref
  8.0 2.1 shard_map.73
  10.1 36.8 %all-gather = f32[512,128]{1,0:T(8,128)} all-gather(f32[16,128]{1,0:T(8,128)} %get-tuple-element.8), channel_id=2, replica_groups=mesh['ctx'=32,'tp'=32] {'ctx'}, dimensions={0}, use_global_device_ids=true | all-gather | bytes 270336 | tf_op jit(solution)/shard_map/all_gather | solution.py:84
  46.9 3.0 %shard_map.74 = bf16[512,128]{1,0:T(8,128)(2,1)} custom-call(s32[1]{0:T(128)} %bitcast.index_ref, f32[32,16,128]{2,1,0:T(8,128)} %bitcast.9, f32[128,128]{1,0:T(8,128)} %get-tuple-element.9.chunk_ref, f32[16,128]{1,0:T(8,128)} %rate_ref.3, f32[16,128]{1,0:T(8,128)} %sqrt_multiply_fusion.weight_ref, f32[1,128]{1,0:T(1,128)} %bitcast.10, ...), custom_call_target="tpu_custom_call" | custom-call | tf_op jit(solution)/shard_map/pallas_call | solution.py:87
  49.9 0.0 copy-done
  49.9 5.4 %convolution_bitcast_fusion = f32[4096,512]{0,1:T(8,128)} fusion(bf16[512,128]{1,0:T(8,128)(2,1)} %shard_map.74, bf16[128,4096]{1,0:T(8,128)(2,1)S(1)} %copy-done), kind=kOutput, calls=%fused_computation | convolution fusion | flops 536870912 | bytes 9568256 | tf_op jit(solution)/shard_map/dot_general | solution.py:99
  55.3 0.0 reduce-scatter.2.cloned.1.call-update
  55.3 150.3 %reduce-scatter.2.cloned.1.call-done = f32[128,512]{0,1:T(8,128)} async-done(((f32[4096,512]{0,1:T(8,128)}), f32[128,512]{0,1:T(8,128)}) %reduce-scatter.2.cloned.1.call-update) | async-done | bytes 262160 | tf_op jit(solution)/shard_map/reduce_scatter | solution.py:98
  205.6 1.6 convert_bitcast_fusion
Async XLA Ops:
  6.5 43.4 %copy-start = (bf16[128,4096]{1,0:T(8,128)(2,1)S(1)}, bf16[128,4096]{1,0:T(8,128)(2,1)}, u32[]{:S(2)}) copy-start(bf16[128,4096]{1,0:T(8,128)(2,1)} %param.13) | copy-start | bytes 3145732
  6.5 199.1 %reduce-scatter.2.cloned.1.call-start = ((), (), s32[]{:S(2)}) async-start(), calls=%async_computation.1 | async-start | bytes 8650752 | tf_op jit(solution)/shard_map/reduce_scatter | solution.py:98
Sparse Core Ops, SparseCore 0:
  55.4 150.1 reduce-scatter.1

commit v2 on v1

v2 whole, which is shorter than its diff:
```python
import functools

import jax
import jax.numpy as jnp
from jax import lax
from jax.experimental import pallas as pl
from jax.experimental.pallas import tpu as pltpu
from jax.sharding import PartitionSpec as P

chunks = 8


def mode_rows(values, mode_count):
    return [jnp.broadcast_to(values[m : m + 1, :], (chunks, values.shape[1])) for m in range(mode_count)]


def one_minus_exp(x):
    series = jnp.ones_like(x)
    for k in range(9, 1, -1):
        series = 1.0 - x * series * (1.0 / k)
    return jnp.where(x < 0.25, x * series, 1.0 - jnp.exp(-x))


def states_kernel(key_ref, value_ref, rate_ref, chunk_ref, end_ref, signal_ref):
    modes = rate_ref.shape[0]
    steps = key_ref.shape[0] // chunks
    signal_ref[...] = key_ref[...].astype(jnp.float32) * value_ref[...].astype(jnp.float32)
    rates = rate_ref[...]
    decays = mode_rows(jnp.exp(-rates), modes)

    def step(t, states):
        x = signal_ref[pl.ds(t, chunks, stride=steps), :]
        return tuple(decays[m] * states[m] + x for m in range(modes))

    zero = jnp.zeros((chunks, rates.shape[1]), jnp.float32)
    states = lax.fori_loop(0, steps, step, (zero,) * modes, unroll=8)
    for m in range(modes):
        chunk_ref[pl.ds(m, chunks, stride=modes), :] = states[m]
    chunk_decay = jnp.exp(-float(steps) * rates)
    end = jnp.zeros_like(rates)
    for c in range(chunks):
        end = chunk_decay * end + chunk_ref[c * modes : (c + 1) * modes, :]
    end_ref[...] = jnp.broadcast_to(end[None], end_ref.shape)


def product_kernel(
    index_ref,
    ends_ref,
    chunk_ref,
    rate_ref,
    residue_ref,
    skip_ref,
    query_ref,
    signal_ref,
    out_weight_ref,
    product_ref,
    start_ref,
    wide_ref,
    shifted_ref,
):
    modes = rate_ref.shape[0]
    length, width = query_ref.shape
    steps = length // chunks
    index = index_ref[0]
    rates = rate_ref[...]
    block_decay = jnp.exp(-float(length) * rates)
    carry = jnp.zeros_like(rates)
    for d in range(ends_ref.shape[0]):
        carry = jnp.where(d < index, block_decay * carry + ends_ref[d], carry)
    chunk_decay = jnp.exp(-float(steps) * rates)
    for c in range(chunks):
        rows = slice(c * modes, (c + 1) * modes)
        start_ref[rows, :] = carry
        carry = chunk_decay * carry + chunk_ref[rows, :]
    decays = mode_rows(jnp.exp(-rates), modes)
    weights = mode_rows(residue_ref[...] * jnp.sqrt(one_minus_exp(2.0 * rates)), modes)
    skip = jnp.broadcast_to(skip_ref[...], (chunks, width))
    wide_ref[...] = query_ref[...].astype(jnp.float32)

    def step(t, states):
        rows = pl.ds(t, chunks, stride=steps)
        x = signal_ref[rows, :]
        after = tuple(decays[m] * states[m] + x for m in range(modes))
        terms = [weights[m] * after[m] for m in range(modes)]
        while len(terms) > 1:
            terms = [terms[i] + terms[i + 1] for i in range(0, len(terms), 2)]
        wide_ref[rows, :] = wide_ref[rows, :] * (terms[0] + skip * x)
        return after

    states = tuple(start_ref[pl.ds(m, chunks, stride=modes), :] for m in range(modes))
    lax.fori_loop(0, steps, step, states, unroll=4)

    groups = out_weight_ref.shape[1] // width
    block = product_ref.shape[0] // groups
    shifted_ref[...] = jnp.zeros_like(shifted_ref)
    for first in range(8):
        shift = first * block % 8
        shifted_ref[0:8, :] = jnp.zeros((8, width), jnp.float32)
        shifted_ref[shift : shift + length, :] = wide_ref[...].astype(jnp.bfloat16).astype(jnp.float32)
        shifted_ref[length + shift : length + 16, :] = jnp.zeros((16 - shift, width), jnp.float32)
        left = shifted_ref[...].astype(jnp.bfloat16)
        members = range(first, groups, 8)
        right = jnp.concatenate([out_weight_ref[:, g * width : (g + 1) * width] for g in members], axis=1)
        both = jnp.dot(left, right, preferred_element_type=jnp.float32)
        for place, g in enumerate(members):
            base = g * block - shift
            rows = (g + 1) * block - (first + 1) * block % 8 - base
            product_ref[base : base + rows, :] = both[:rows, place * width : (place + 1) * width]


def round_kernel(summed_ref, mixed_ref):
    mixed_ref[...] = summed_ref[: mixed_ref.shape[0], :].astype(jnp.bfloat16)


def per_device(query, key_proj, value, decay_rates, residues, skip_gain, out_weight):
    length, width = query.shape
    modes = decay_rates.shape[0]
    groups = out_weight.shape[1] // width
    block = length + 15
    shape = functools.partial(jax.ShapeDtypeStruct, dtype=jnp.float32)
    vmem = pl.BlockSpec(memory_space=pltpu.VMEM)
    chunk_states, end_state, signal = pl.pallas_call(
        states_kernel,
        out_shape=(shape((chunks * modes, width)), shape((lax.axis_size("ctx"), modes, width)), shape((length, width))),
    )(key_proj, value, decay_rates)
    ends = lax.all_to_all(end_state, "ctx", split_axis=0, concat_axis=0)
    product = pl.pallas_call(
        product_kernel,
        out_shape=shape((groups * block, width)),
        in_specs=[pl.BlockSpec(memory_space=pltpu.SMEM)] + [vmem] * 8,
        out_specs=vmem,
        scratch_shapes=[
            pltpu.VMEM((chunks * modes, width), jnp.float32),
            pltpu.VMEM((length, width), jnp.float32),
            pltpu.VMEM((length + 16, width), jnp.float32),
        ],
        compiler_params=pltpu.CompilerParams(vmem_limit_bytes=40 * 1024 * 1024),
    )(
        lax.axis_index("ctx").reshape(1),
        ends,
        chunk_states,
        decay_rates,
        residues,
        skip_gain[None, :],
        query,
        signal,
        out_weight,
    )
    summed = lax.psum_scatter(product, "tp", scatter_dimension=0, tiled=True)
    return pl.pallas_call(round_kernel, out_shape=jax.ShapeDtypeStruct((length, width), jnp.bfloat16))(summed)


def solution(mesh):
    placed = (
        P("ctx", "tp"),
        P("ctx", "tp"),
        P("ctx", "tp"),
        P(None, "tp"),
        P(None, "tp"),
        P("tp"),
        P("tp", None),
    )
    return jax.shard_map(
        per_device, mesh=mesh, in_specs=placed, out_specs=P("ctx", "tp"), check_vma=False
    )
```

time: 214 us -> 154 us (0.72)
  waiting for transfers between devices: 150 us -> 7.09 us
  blocking collectives: 36.8 us -> 107 us
  starting transfers between devices: 0.01 us -> 19.3 us
  between operations: 13.4 us -> 0.73 us
  local copies, waits for them, and re-layouts: 0.01 us -> 12 us
  matrix products: 5.37 us -> 0 us
  other arithmetic: 3.04 us -> 0 us
    reduce_scatter x1 -> x0, waiting for transfers between devices: 150 us -> none  [per_device(): lax.psum_scatter(lax.dot_general(out_weight, gated, (((0,), (1,)), ((), (...]
    unnamed x0 -> x1, blocking collectives: none -> 107 us
    all_gather x1 -> x0, blocking collectives: 36.8 us -> none  [gated_block(): ends = lax.all_gather(end_state, 'ctx')]
    all_to_all x0 -> x1, starting transfers between devices: none -> 16.7 us  [per_device(): ends = lax.all_to_all(end_state, 'ctx', split_axis=0, concat_axis=0)]
    unnamed x2 -> x20, local copies, waits for them, and re-layouts: 0.01 us -> 12 us
    all_to_all x0 -> x1, waiting for transfers between devices: none -> 7.09 us  [per_device(): ends = lax.all_to_all(end_state, 'ctx', split_axis=0, concat_axis=0)]
    dot_general x1 -> x0, matrix products: 5.37 us -> none  [per_device(): lax.dot_general(out_weight, gated, (((0,), (1,)), ((), ())), preferred_el...]
    unnamed x0 -> x1, starting transfers between devices: none -> 2.66 us
  transfers between devices with their start and end apart: 1 -> 2, of which waited for: 1 -> 1; matrix products, arithmetic and copies ran while one was open for 0% -> 1% of each run, Pallas kernels for 0% -> 0%
where the time goes in v2:
time: 154 us; the launch traced here: 153 us
  blocking collectives  107 us (69%)
  starting transfers between devices  19.3 us (13%)
  local copies, waits for them, and re-layouts  12 us (8%)
  waiting for transfers between devices  7.09 us (5%)
  Pallas kernels  6.29 us (4%)
    unnamed x1, blocking collectives  107 us
    all_to_all x1, starting transfers between devices, per_device(): ends = lax.all_to_all(end_state, 'ctx', split_axis=0, concat_axis=0)  16.7 us
    unnamed x20, local copies, waits for them, and re-layouts  12 us
    all_to_all x1, waiting for transfers between devices, per_device(): ends = lax.all_to_all(end_state, 'ctx', split_axis=0, concat_axis=0)  7.09 us
  transfers between devices with their start and end apart: 2, of which 1 were waited for; matrix products, arithmetic and copies ran while one was open for 1% of the time, Pallas kernels for 0%

profile of v2, /device:TPU:6, one launch (start us, length us, event | category | flops | bytes accessed | tf_op | source)
XLA Modules:
  0.0 152.5 jit_solution(5339716649540979999)
XLA Ops:
  0.0 2.2 %shard_map.73 = (f32[128,128]{1,0:T(8,128)}, f32[32,16,128]{2,1,0:T(8,128)}, f32[512,128]{1,0:T(8,128)}) custom-call(bf16[512,128]{1,0:T(8,128)(2,1)} %key_ref.1, bf16[512,128]{1,0:T(8,128)(2,1)} %value_ref.1, f32[16,128]{1,0:T(8,128)} %rate_ref.3), custom_call_target="tpu_custom_call" | custom-call | tf_op jit(solution)/shard_map/pallas_call | solution.py:122
  2.2 16.7 %all-to-all-start = ((f32[32,16,128]{2,1,0:T(8,128)}), f32[32,16,128]{2,1,0:T(8,128)S(1)}, u32[]{:S(2)}, u32[]{:S(2)}) async-start(f32[32,16,128]{2,1,0:T(8,128)} %get-tuple-element.8), calls=%async_computation | async-start | bytes 524288 | tf_op jit(solution)/shard_map/all_to_all | solution.py:126
  18.9 7.1 %all-to-all-done.ends_ref = f32[32,16,128]{2,1,0:T(8,128)S(1)} async-done(((f32[32,16,128]{2,1,0:T(8,128)}), f32[32,16,128]{2,1,0:T(8,128)S(1)}, u32[]{:S(2)}, u32[]{:S(2)}) %all-to-all-start) | async-done | bytes 262176 | tf_op jit(solution)/shard_map/all_to_all | solution.py:126
  26.0 0.0 copy-start.1
  26.0 1.2 copy-done.1
  27.2 0.0 copy-start.2
  27.3 0.9 copy-done.2
  28.2 0.0 copy-start.3
  28.2 0.9 copy-done.3
  29.1 0.0 copy-start.4
  29.1 0.8 copy-done.4
  29.9 0.0 copy-start.5
  29.9 0.7 copy-done.5
  30.6 0.0 copy-start.6
  30.6 0.7 copy-done.6
  31.3 0.0 copy-start.7
  31.3 0.7 copy-done.7
  32.0 2.4 %shard_map.74 = f32[16864,128]{1,0:T(8,128)S(1)} custom-call(s32[1]{0:T(128)} %bitcast.index_ref, f32[32,16,128]{2,1,0:T(8,128)S(1)} %all-to-all-done.ends_ref, f32[128,128]{1,0:T(8,128)S(1)} %copy-done.4, f32[16,128]{1,0:T(8,128)S(1)} %copy-done.5, f32[16,128]{1,0:T(8,128)S(1)} %copy-done.6, f32[1,128]{1,0:T(1,128)S(1)} %bitcast.5, ...), custom_call_target="tpu_custom_call" | custom-call | tf_op jit(solution)/shard_map/pallas_call | solution.py:127
  34.4 0.0 copy-start
  34.4 3.3 %copy-done = f32[16864,128]{1,0:T(8,128)} copy-done((f32[16864,128]{1,0:T(8,128)}, f32[16864,128]{1,0:T(8,128)S(1)}, u32[]{:S(2)}) %copy-start) | copy-done | bytes 8634392
  37.8 107.1 %fusion = f32[528,128]{1,0:T(8,128)S(1)} fusion(f32[16864,128]{1,0:T(8,128)} %copy-done), kind=kCustom, calls=%all-reduce-scatter | all-reduce-scatter fusion | flops 2162689 | bytes 8908800
  144.8 2.7 %collective-permute-start = (f32[31,128]{1,0:T(8,128)S(1)}, f32[31,128]{1,0:T(8,128)S(1)}, u32[]{:S(2)}, u32[]{:S(2)}) collective-permute-start(f32[31,128]{1,0:T(8,128)S(1)} %slice), channel_id=1, source_target_pairs={{0,1},{1,2},{2,3},{3,4},{4,5},{5,6},{6,7},{7,8},{8,9},{9,10},{10,1... | collective-permute-start | bytes 47624
  147.5 1.3 dynamic-slice.4
  149.4 0.0 collective-permute-done
  149.4 0.7 concatenate
  150.2 0.7 constant_dynamic-slice_fusion.summed_ref
  150.9 1.6 %shard_map.75 = bf16[512,128]{1,0:T(8,128)(2,1)} custom-call(f32[527,128]{1,0:T(8,128)} %constant_dynamic-slice_fusion.summed_ref), custom_call_target="tpu_custom_call" | custom-call | tf_op jit(solution)/shard_map/pallas_call | solution.py:150
  (1 shorter events, 0.0 us)
Async XLA Ops:
  2.2 23.8 %all-to-all-start = ((f32[32,16,128]{2,1,0:T(8,128)}), f32[32,16,128]{2,1,0:T(8,128)S(1)}, u32[]{:S(2)}, u32[]{:S(2)}) async-start(f32[32,16,128]{2,1,0:T(8,128)} %get-tuple-element.8), calls=%async_computation | async-start | bytes 524288 | tf_op jit(solution)/shard_map/all_to_all | solution.py:126
  26.0 1.2 copy-start.1
  27.2 0.9 copy-start.2
  28.2 0.9 copy-start.3
  29.1 0.8 copy-start.4
  29.9 0.7 copy-start.5
  30.6 0.7 copy-start.6
  31.3 0.7 copy-start.7
  34.4 3.3 %copy-start = (f32[16864,128]{1,0:T(8,128)}, f32[16864,128]{1,0:T(8,128)S(1)}, u32[]{:S(2)}) copy-start(f32[16864,128]{1,0:T(8,128)S(1)} %shard_map.74) | copy-start | bytes 25903108
  144.8 4.6 %collective-permute-start = (f32[31,128]{1,0:T(8,128)S(1)}, f32[31,128]{1,0:T(8,128)S(1)}, u32[]{:S(2)}, u32[]{:S(2)}) collective-permute-start(f32[31,128]{1,0:T(8,128)S(1)} %slice), channel_id=1, source_target_pairs={{0,1},{1,2},{2,3},{3,4},{4,5},{5,6},{6,7},{7,8},{8,9},{9,10},{10,1... | collective-permute-start | bytes 47624

commit v3 on v2

--- a/solution.py
+++ b/solution.py
@@ -51,13 +51,21 @@
     residue_ref,
     skip_ref,
     query_ref,
+    key_ref,
+    value_ref,
+    out_weight_hbm,
+    product_hbm,
+    start_ref,
+    wide_ref,
     signal_ref,
+    shifted_ref,
     out_weight_ref,
     product_ref,
-    start_ref,
-    wide_ref,
-    shifted_ref,
+    load_sem,
+    store_sems,
 ):
+    load = pltpu.make_async_copy(out_weight_hbm, out_weight_ref, load_sem)
+    load.start()
     modes = rate_ref.shape[0]
     length, width = query_ref.shape
     steps = length // chunks
@@ -76,6 +84,7 @@
     weights = mode_rows(residue_ref[...] * jnp.sqrt(one_minus_exp(2.0 * rates)), modes)
     skip = jnp.broadcast_to(skip_ref[...], (chunks, width))
     wide_ref[...] = query_ref[...].astype(jnp.float32)
+    signal_ref[...] = key_ref[...].astype(jnp.float32) * value_ref[...].astype(jnp.float32)
 
     def step(t, states):
         rows = pl.ds(t, chunks, stride=steps)
@@ -90,6 +99,8 @@
     states = tuple(start_ref[pl.ds(m, chunks, stride=modes), :] for m in range(modes))
     lax.fori_loop(0, steps, step, states, unroll=4)
 
+    load.wait()
+    stores = []
     groups = out_weight_ref.shape[1] // width
     block = product_ref.shape[0] // groups
     shifted_ref[...] = jnp.zeros_like(shifted_ref)
@@ -101,15 +112,18 @@
         left = shifted_ref[...].astype(jnp.bfloat16)
         members = range(first, groups, 8)
         right = jnp.concatenate([out_weight_ref[:, g * width : (g + 1) * width] for g in members], axis=1)
-        both = jnp.dot(left, right, preferred_element_type=jnp.float32)
+        both = 0.5 * jnp.dot(left, right, preferred_element_type=jnp.float32)
         for place, g in enumerate(members):
             base = g * block - shift
             rows = (g + 1) * block - (first + 1) * block % 8 - base
             product_ref[base : base + rows, :] = both[:rows, place * width : (place + 1) * width]
-
-
-def round_kernel(summed_ref, mixed_ref):
-    mixed_ref[...] = summed_ref[: mixed_ref.shape[0], :].astype(jnp.bfloat16)
+            store = pltpu.make_async_copy(
+                product_ref.at[pl.ds(base, rows), :], product_hbm.at[pl.ds(base, rows), :], store_sems.at[g]
+            )
+            store.start()
+            stores.append(store)
+    for store in stores:
+        store.wait()
 
 
 def per_device(query, key_proj, value, decay_rates, residues, skip_gain, out_weight):
@@ -119,22 +133,28 @@
     block = length + 15
     shape = functools.partial(jax.ShapeDtypeStruct, dtype=jnp.float32)
     vmem = pl.BlockSpec(memory_space=pltpu.VMEM)
-    chunk_states, end_state, signal = pl.pallas_call(
+    chunk_states, end_state = pl.pallas_call(
         states_kernel,
-        out_shape=(shape((chunks * modes, width)), shape((lax.axis_size("ctx"), modes, width)), shape((length, width))),
+        out_shape=(shape((chunks * modes, width)), shape((lax.axis_size("ctx"), modes, width))),
+        scratch_shapes=[pltpu.VMEM((length, width), jnp.float32)],
     )(key_proj, value, decay_rates)
     ends = lax.all_to_all(end_state, "ctx", split_axis=0, concat_axis=0)
     product = pl.pallas_call(
         product_kernel,
         out_shape=shape((groups * block, width)),
-        in_specs=[pl.BlockSpec(memory_space=pltpu.SMEM)] + [vmem] * 8,
-        out_specs=vmem,
+        in_specs=[pl.BlockSpec(memory_space=pltpu.SMEM)] + [vmem] * 8 + [pl.BlockSpec(memory_space=pl.ANY)],
+        out_specs=pl.BlockSpec(memory_space=pl.ANY),
         scratch_shapes=[
             pltpu.VMEM((chunks * modes, width), jnp.float32),
             pltpu.VMEM((length, width), jnp.float32),
+            pltpu.VMEM((length, width), jnp.float32),
             pltpu.VMEM((length + 16, width), jnp.float32),
+            pltpu.VMEM(out_weight.shape, jnp.bfloat16),
+            pltpu.VMEM((groups * block, width), jnp.float32),
+            pltpu.SemaphoreType.DMA,
+            pltpu.SemaphoreType.DMA((groups,)),
         ],
-        compiler_params=pltpu.CompilerParams(vmem_limit_bytes=40 * 1024 * 1024),
+        compiler_params=pltpu.CompilerParams(vmem_limit_bytes=60 * 1024 * 1024),
     )(
         lax.axis_index("ctx").reshape(1),
         ends,
@@ -143,11 +163,12 @@
         residues,
         skip_gain[None, :],
         query,
-        signal,
+        key_proj,
+        value,
         out_weight,
     )
-    summed = lax.psum_scatter(product, "tp", scatter_dimension=0, tiled=True)
-    return pl.pallas_call(round_kernel, out_shape=jax.ShapeDtypeStruct((length, width), jnp.bfloat16))(summed)
+    summed = lax.optimization_barrier(lax.psum_scatter(product, "tp", scatter_dimension=0, tiled=True))
+    return (2.0 * summed[:length]).astype(jnp.bfloat16)
 
 
 def solution(mesh):

time: 154 us -> 148 us (0.961)
  local copies, waits for them, and re-layouts: 12 us -> 2.72 us
  Pallas kernels: 6.29 us -> 8.47 us
    unnamed x20 -> x6, local copies, waits for them, and re-layouts: 12 us -> 2.72 us
    pallas_call x1, Pallas kernels: 2.43 us -> 6.32 us  [per_device(): pl.pallas_call(product_kernel, out_shape=shape((groups * block, width)),...]
    pallas_call x1 -> x0, Pallas kernels: 1.62 us -> none  [per_device(): pl.pallas_call(round_kernel, out_shape=jax.ShapeDtypeStruct((length, widt...]
where the time goes in v3:
time: 148 us; the launch traced here: 146 us
  blocking collectives  107 us (72%)
  starting transfers between devices  19.3 us (13%)
  Pallas kernels  8.47 us (6%)
  waiting for transfers between devices  7.09 us (5%)
  local copies, waits for them, and re-layouts  2.72 us (2%)
    unnamed x1, blocking collectives  107 us
    all_to_all x1, starting transfers between devices, per_device(): ends = lax.all_to_all(end_state, 'ctx', split_axis=0, concat_axis=0)  16.7 us
    all_to_all x1, waiting for transfers between devices, per_device(): ends = lax.all_to_all(end_state, 'ctx', split_axis=0, concat_axis=0)  7.09 us
    pallas_call x1, Pallas kernels, per_device(): pl.pallas_call(product_kernel, out_shape=shape((groups * block, width)),...  6.32 us
  transfers between devices with their start and end apart: 2, of which 1 were waited for; matrix products, arithmetic and copies ran while one was open for 1% of the time, Pallas kernels for 0%

profile of v3, /device:TPU:6, one launch (start us, length us, event | category | flops | bytes accessed | tf_op | source)
XLA Modules:
  0.0 146.1 jit_solution(706185041533192753)
XLA Ops:
  0.0 2.1 %shard_map.73 = (f32[128,128]{1,0:T(8,128)}, f32[32,16,128]{2,1,0:T(8,128)}) custom-call(bf16[512,128]{1,0:T(8,128)(2,1)} %key_ref.3, bf16[512,128]{1,0:T(8,128)(2,1)} %value_ref.3, f32[16,128]{1,0:T(8,128)} %rate_ref.3), custom_call_target="tpu_custom_call" | custom-call | tf_op jit(solution)/shard_map/pallas_call | solution.py:136
  2.1 16.7 %all-to-all-start = ((f32[32,16,128]{2,1,0:T(8,128)}), f32[32,16,128]{2,1,0:T(8,128)S(1)}, u32[]{:S(2)}, u32[]{:S(2)}) async-start(f32[32,16,128]{2,1,0:T(8,128)} %get-tuple-element.7), calls=%async_computation | async-start | bytes 524288 | tf_op jit(solution)/shard_map/all_to_all | solution.py:141
  18.8 7.1 %all-to-all-done.ends_ref = f32[32,16,128]{2,1,0:T(8,128)S(1)} async-done(((f32[32,16,128]{2,1,0:T(8,128)}), f32[32,16,128]{2,1,0:T(8,128)S(1)}, u32[]{:S(2)}, u32[]{:S(2)}) %all-to-all-start) | async-done | bytes 262176 | tf_op jit(solution)/shard_map/all_to_all | solution.py:141
  25.9 0.0 copy-start
  25.9 0.7 copy-done
  26.6 6.3 %shard_map.74 = f32[16864,128]{1,0:T(8,128)} custom-call(s32[1]{0:T(128)} %bitcast.index_ref, f32[32,16,128]{2,1,0:T(8,128)} %copy-done, f32[128,128]{1,0:T(8,128)} %get-tuple-element.8.chunk_ref, f32[16,128]{1,0:T(8,128)} %rate_ref.3, f32[16,128]{1,0:T(8,128)} %residue_ref.1, f32[1,128]{1,0:T(1,128)} %bitcast.5, bf16[512,128]{1,0:T(8,128)(2,1)} %query_ref.1, ...), custom_call_target="tpu_custom_call" | custom-call | tf_op jit(solution)/shard_map/pallas_call | solution.py:142
  33.0 107.1 %fusion = f32[528,128]{1,0:T(8,128)S(1)} fusion(f32[16864,128]{1,0:T(8,128)} %shard_map.74), kind=kCustom, calls=%all-reduce-scatter | all-reduce-scatter fusion | flops 2162689 | bytes 8908800
  140.0 2.7 %collective-permute-start = (f32[31,128]{1,0:T(8,128)S(1)}, f32[31,128]{1,0:T(8,128)S(1)}, u32[]{:S(2)}, u32[]{:S(2)}) collective-permute-start(f32[31,128]{1,0:T(8,128)S(1)} %slice.5), channel_id=1, source_target_pairs={{0,1},{1,2},{2,3},{3,4},{4,5},{5,6},{6,7},{7,8},{8,9},{9,10},{10,1... | collective-permute-start | bytes 47624
  142.7 1.3 dynamic-slice.4
  144.6 0.0 collective-permute-done
  144.6 0.7 concatenate
  145.4 0.7 fusion.1
  (2 shorter events, 0.0 us)
Async XLA Ops:
  2.1 23.8 %all-to-all-start = ((f32[32,16,128]{2,1,0:T(8,128)}), f32[32,16,128]{2,1,0:T(8,128)S(1)}, u32[]{:S(2)}, u32[]{:S(2)}) async-start(f32[32,16,128]{2,1,0:T(8,128)} %get-tuple-element.7), calls=%async_computation | async-start | bytes 524288 | tf_op jit(solution)/shard_map/all_to_all | solution.py:141
  25.9 0.7 copy-start
  140.0 4.6 %collective-permute-start = (f32[31,128]{1,0:T(8,128)S(1)}, f32[31,128]{1,0:T(8,128)S(1)}, u32[]{:S(2)}, u32[]{:S(2)}) collective-permute-start(f32[31,128]{1,0:T(8,128)S(1)} %slice.5), channel_id=1, source_target_pairs={{0,1},{1,2},{2,3},{3,4},{4,5},{5,6},{6,7},{7,8},{8,9},{9,10},{10,1... | collective-permute-start | bytes 47624

commit v4 on v3

--- a/solution.py
+++ b/solution.py
@@ -130,7 +130,7 @@
     length, width = query.shape
     modes = decay_rates.shape[0]
     groups = out_weight.shape[1] // width
-    block = length + 15
+    block = length + 7
     shape = functools.partial(jax.ShapeDtypeStruct, dtype=jnp.float32)
     vmem = pl.BlockSpec(memory_space=pltpu.VMEM)
     chunk_states, end_state = pl.pallas_call(

time: 148 us -> 150 us (1.014)
  transfers between devices with their start and end apart: 2 -> 2, of which waited for: 1 -> 2; matrix products, arithmetic and copies ran while one was open for 1% -> 1% of each run, Pallas kernels for 0% -> 0%
where the time goes in v4:
time: 150 us; the launch traced here: 148 us
  blocking collectives  107 us (71%)
  starting transfers between devices  20.6 us (14%)
  Pallas kernels  8.43 us (6%)
  waiting for transfers between devices  7.77 us (5%)
  local copies, waits for them, and re-layouts  2.77 us (2%)
    unnamed x1, blocking collectives  107 us
    all_to_all x1, starting transfers between devices, per_device(): ends = lax.all_to_all(end_state, 'ctx', split_axis=0, concat_axis=0)  16.7 us
    all_to_all x1, waiting for transfers between devices, per_device(): ends = lax.all_to_all(end_state, 'ctx', split_axis=0, concat_axis=0)  7.09 us
    pallas_call x1, Pallas kernels, per_device(): pl.pallas_call(product_kernel, out_shape=shape((groups * block, width)),...  6.28 us
    unnamed x1, starting transfers between devices  3.94 us
  transfers between devices with their start and end apart: 2, of which 2 were waited for; matrix products, arithmetic and copies ran while one was open for 1% of the time, Pallas kernels for 0%

profile of v4, /device:TPU:6, one launch (start us, length us, event | category | flops | bytes accessed | tf_op | source)
XLA Modules:
  0.0 148.0 jit_solution(3936178766235826396)
XLA Ops:
  0.0 2.1 %shard_map.73 = (f32[128,128]{1,0:T(8,128)}, f32[32,16,128]{2,1,0:T(8,128)}) custom-call(bf16[512,128]{1,0:T(8,128)(2,1)} %key_ref.3, bf16[512,128]{1,0:T(8,128)(2,1)} %value_ref.3, f32[16,128]{1,0:T(8,128)} %rate_ref.3), custom_call_target="tpu_custom_call" | custom-call | tf_op jit(solution)/shard_map/pallas_call | solution.py:136
  2.1 16.7 %all-to-all-start = ((f32[32,16,128]{2,1,0:T(8,128)}), f32[32,16,128]{2,1,0:T(8,128)S(1)}, u32[]{:S(2)}, u32[]{:S(2)}) async-start(f32[32,16,128]{2,1,0:T(8,128)} %get-tuple-element.7), calls=%async_computation | async-start | bytes 524288 | tf_op jit(solution)/shard_map/all_to_all | solution.py:141
  18.8 7.1 %all-to-all-done.ends_ref = f32[32,16,128]{2,1,0:T(8,128)S(1)} async-done(((f32[32,16,128]{2,1,0:T(8,128)}), f32[32,16,128]{2,1,0:T(8,128)S(1)}, u32[]{:S(2)}, u32[]{:S(2)}) %all-to-all-start) | async-done | bytes 262176 | tf_op jit(solution)/shard_map/all_to_all | solution.py:141
  25.9 0.0 copy-start
  25.9 0.7 copy-done
  26.7 6.3 %shard_map.74 = f32[16608,128]{1,0:T(8,128)} custom-call(s32[1]{0:T(128)} %bitcast.index_ref, f32[32,16,128]{2,1,0:T(8,128)} %copy-done, f32[128,128]{1,0:T(8,128)} %get-tuple-element.8.chunk_ref, f32[16,128]{1,0:T(8,128)} %rate_ref.3, f32[16,128]{1,0:T(8,128)} %residue_ref.1, f32[1,128]{1,0:T(1,128)} %bitcast.5, bf16[512,128]{1,0:T(8,128)(2,1)} %query_ref.1, ...), custom_call_target="tpu_custom_call" | custom-call | tf_op jit(solution)/shard_map/pallas_call | solution.py:142
  33.0 107.1 %fusion = f32[528,128]{1,0:T(8,128)S(1)} fusion(f32[16608,128]{1,0:T(8,128)} %shard_map.74), kind=kCustom, calls=%all-reduce-scatter | all-reduce-scatter fusion | flops 2162689 | bytes 8777728
  140.0 3.9 %collective-permute-start = (f32[279,128]{1,0:T(8,128)S(1)}, f32[279,128]{1,0:T(8,128)S(1)}, u32[]{:S(2)}, u32[]{:S(2)}) collective-permute-start(f32[279,128]{1,0:T(8,128)S(1)} %slice.5), channel_id=1, source_target_pairs={{0,1},{1,2},{2,3},{3,4},{4,5},{5,6},{6,7},{7,8},{8,9},{9,10},{10,1... | collective-permute-start | bytes 428552
  144.0 1.3 dynamic-slice.4
  145.9 0.7 collective-permute-done
  146.6 0.7 concatenate
  147.4 0.7 fusion.1
  (2 shorter events, 0.0 us)
Async XLA Ops:
  2.1 23.8 %all-to-all-start = ((f32[32,16,128]{2,1,0:T(8,128)}), f32[32,16,128]{2,1,0:T(8,128)S(1)}, u32[]{:S(2)}, u32[]{:S(2)}) async-start(f32[32,16,128]{2,1,0:T(8,128)} %get-tuple-element.7), calls=%async_computation | async-start | bytes 524288 | tf_op jit(solution)/shard_map/all_to_all | solution.py:141
  25.9 0.7 copy-start
  140.0 6.6 %collective-permute-start = (f32[279,128]{1,0:T(8,128)S(1)}, f32[279,128]{1,0:T(8,128)S(1)}, u32[]{:S(2)}, u32[]{:S(2)}) collective-permute-start(f32[279,128]{1,0:T(8,128)S(1)} %slice.5), channel_id=1, source_target_pairs={{0,1},{1,2},{2,3},{3,4},{4,5},{5,6},{6,7},{7,8},{8,9},{9,10},{10,1... | collective-permute-start | bytes 428552

commit v5 on v3

--- a/solution.py
+++ b/solution.py
@@ -43,21 +43,55 @@
     end_ref[...] = jnp.broadcast_to(end[None], end_ref.shape)
 
 
+def tree_sum(terms):
+    while len(terms) > 1:
+        terms = [terms[i] + terms[i + 1] for i in range(0, len(terms), 2)]
+    return terms[0]
+
+
+def local_kernel(
+    chunk_ref, rate_ref, residue_ref, skip_ref, query_ref, key_ref, value_ref, local_ref, weight_ref, start_ref, signal_ref
+):
+    modes = rate_ref.shape[0]
+    length, width = query_ref.shape
+    steps = length // chunks
+    rates = rate_ref[...]
+    chunk_decay = jnp.exp(-float(steps) * rates)
+    carry = jnp.zeros_like(rates)
+    for c in range(chunks):
+        rows = slice(c * modes, (c + 1) * modes)
+        start_ref[rows, :] = carry
+        carry = chunk_decay * carry + chunk_ref[rows, :]
+    one_step = jnp.exp(-rates)
+    weight = residue_ref[...] * jnp.sqrt(one_minus_exp(2.0 * rates))
+    weight_ref[...] = weight * one_step
+    decays = mode_rows(one_step, modes)
+    weights = mode_rows(weight, modes)
+    skip = jnp.broadcast_to(skip_ref[...], (chunks, width))
+    signal_ref[...] = key_ref[...].astype(jnp.float32) * value_ref[...].astype(jnp.float32)
+
+    def step(t, states):
+        rows = pl.ds(t, chunks, stride=steps)
+        x = signal_ref[rows, :]
+        after = tuple(decays[m] * states[m] + x for m in range(modes))
+        local_ref[rows, :] = tree_sum([weights[m] * after[m] for m in range(modes)]) + skip * x
+        return after
+
+    states = tuple(start_ref[pl.ds(m, chunks, stride=modes), :] for m in range(modes))
+    lax.fori_loop(0, steps, step, states, unroll=4)
+
+
 def product_kernel(
     index_ref,
     ends_ref,
-    chunk_ref,
     rate_ref,
-    residue_ref,
-    skip_ref,
+    weight_ref,
     query_ref,
-    key_ref,
-    value_ref,
+    local_ref,
     out_weight_hbm,
     product_hbm,
     start_ref,
-    wide_ref,
-    signal_ref,
+    conv_ref,
     shifted_ref,
     out_weight_ref,
     product_ref,
@@ -76,28 +110,20 @@
     for d in range(ends_ref.shape[0]):
         carry = jnp.where(d < index, block_decay * carry + ends_ref[d], carry)
     chunk_decay = jnp.exp(-float(steps) * rates)
+    carry = weight_ref[...] * carry
     for c in range(chunks):
-        rows = slice(c * modes, (c + 1) * modes)
-        start_ref[rows, :] = carry
-        carry = chunk_decay * carry + chunk_ref[rows, :]
+        start_ref[c * modes : (c + 1) * modes, :] = carry
+        carry = chunk_decay * carry
     decays = mode_rows(jnp.exp(-rates), modes)
-    weights = mode_rows(residue_ref[...] * jnp.sqrt(one_minus_exp(2.0 * rates)), modes)
-    skip = jnp.broadcast_to(skip_ref[...], (chunks, width))
-    wide_ref[...] = query_ref[...].astype(jnp.float32)
-    signal_ref[...] = key_ref[...].astype(jnp.float32) * value_ref[...].astype(jnp.float32)
-
-    def step(t, states):
+
+    def step(t, tails):
         rows = pl.ds(t, chunks, stride=steps)
-        x = signal_ref[rows, :]
-        after = tuple(decays[m] * states[m] + x for m in range(modes))
-        terms = [weights[m] * after[m] for m in range(modes)]
-        while len(terms) > 1:
-            terms = [terms[i] + terms[i + 1] for i in range(0, len(terms), 2)]
-        wide_ref[rows, :] = wide_ref[rows, :] * (terms[0] + skip * x)
-        return after
-
-    states = tuple(start_ref[pl.ds(m, chunks, stride=modes), :] for m in range(modes))
-    lax.fori_loop(0, steps, step, states, unroll=4)
+        conv_ref[rows, :] = local_ref[rows, :] + tree_sum(list(tails))
+        return tuple(decays[m] * tails[m] for m in range(modes))
+
+    tails = tuple(start_ref[pl.ds(m, chunks, stride=modes), :] for m in range(modes))
+    lax.fori_loop(0, steps, step, tails, unroll=4)
+    conv_ref[...] = ((0.5 * query_ref[...].astype(jnp.float32)) * conv_ref[...]).astype(jnp.bfloat16).astype(jnp.float32)
 
     load.wait()
     stores = []
@@ -107,21 +133,22 @@
     for first in range(8):
         shift = first * block % 8
         shifted_ref[0:8, :] = jnp.zeros((8, width), jnp.float32)
-        shifted_ref[shift : shift + length, :] = wide_ref[...].astype(jnp.bfloat16).astype(jnp.float32)
+        shifted_ref[shift : shift + length, :] = conv_ref[...]
         shifted_ref[length + shift : length + 16, :] = jnp.zeros((16 - shift, width), jnp.float32)
         left = shifted_ref[...].astype(jnp.bfloat16)
         members = range(first, groups, 8)
-        right = jnp.concatenate([out_weight_ref[:, g * width : (g + 1) * width] for g in members], axis=1)
-        both = 0.5 * jnp.dot(left, right, preferred_element_type=jnp.float32)
-        for place, g in enumerate(members):
-            base = g * block - shift
-            rows = (g + 1) * block - (first + 1) * block % 8 - base
-            product_ref[base : base + rows, :] = both[:rows, place * width : (place + 1) * width]
-            store = pltpu.make_async_copy(
-                product_ref.at[pl.ds(base, rows), :], product_hbm.at[pl.ds(base, rows), :], store_sems.at[g]
-            )
-            store.start()
-            stores.append(store)
+        for pair in zip(members[::2], members[1::2]):
+            right = jnp.concatenate([out_weight_ref[:, g * width : (g + 1) * width] for g in pair], axis=1)
+            both = jnp.dot(left, right, preferred_element_type=jnp.float32)
+            for place, g in enumerate(pair):
+                base = g * block - shift
+                rows = (g + 1) * block - (first + 1) * block % 8 - base
+                product_ref[base : base + rows, :] = both[:rows, place * width : (place + 1) * width]
+                store = pltpu.make_async_copy(
+                    product_ref.at[pl.ds(base, rows), :], product_hbm.at[pl.ds(base, rows), :], store_sems.at[g]
+                )
+                store.start()
+                stores.append(store)
     for store in stores:
         store.wait()
 
@@ -139,14 +166,19 @@
         scratch_shapes=[pltpu.VMEM((length, width), jnp.float32)],
     )(key_proj, value, decay_rates)
     ends = lax.all_to_all(end_state, "ctx", split_axis=0, concat_axis=0)
+    local, weights = pl.pallas_call(
+        local_kernel,
+        out_shape=(shape((length, width)), shape((modes, width))),
+        scratch_shapes=[pltpu.VMEM((chunks * modes, width), jnp.float32), pltpu.VMEM((length, width), jnp.float32)],
+        cost_estimate=pl.CostEstimate(flops=70 * length * width, bytes_accessed=5 * length * width * 2, transcendentals=0),
+    )(chunk_states, decay_rates, residues, skip_gain[None, :], query, key_proj, value)
     product = pl.pallas_call(
         product_kernel,
         out_shape=shape((groups * block, width)),
-        in_specs=[pl.BlockSpec(memory_space=pltpu.SMEM)] + [vmem] * 8 + [pl.BlockSpec(memory_space=pl.ANY)],
+        in_specs=[pl.BlockSpec(memory_space=pltpu.SMEM)] + [vmem] * 5 + [pl.BlockSpec(memory_space=pl.ANY)],
         out_specs=pl.BlockSpec(memory_space=pl.ANY),
         scratch_shapes=[
             pltpu.VMEM((chunks * modes, width), jnp.float32),
-            pltpu.VMEM((length, width), jnp.float32),
             pltpu.VMEM((length, width), jnp.float32),
             pltpu.VMEM((length + 16, width), jnp.float32),
             pltpu.VMEM(out_weight.shape, jnp.bfloat16),
@@ -155,18 +187,7 @@
             pltpu.SemaphoreType.DMA((groups,)),
         ],
         compiler_params=pltpu.CompilerParams(vmem_limit_bytes=60 * 1024 * 1024),
-    )(
-        lax.axis_index("ctx").reshape(1),
-        ends,
-        chunk_states,
-        decay_rates,
-        residues,
-        skip_gain[None, :],
-        query,
-        key_proj,
-        value,
-        out_weight,
-    )
+    )(lax.axis_index("ctx").reshape(1), ends, decay_rates, weights, query, local, out_weight)
     summed = lax.optimization_barrier(lax.psum_scatter(product, "tp", scatter_dimension=0, tiled=True))
     return (2.0 * summed[:length]).astype(jnp.bfloat16)
 

time: 148 us -> 148 us (level)
  waiting for transfers between devices: 7.09 us -> 4.35 us
  Pallas kernels: 8.47 us -> 11.1 us
    all_to_all x1, waiting for transfers between devices: 7.09 us -> 4.34 us  [per_device(): ends = lax.all_to_all(end_state, 'ctx', split_axis=0, concat_axis=0)]
    pallas_call x0 -> x1, Pallas kernels: none -> 2.74 us  [per_device(): pl.pallas_call(local_kernel, out_shape=(shape((length, width)), shape((mo...]
  transfers between devices with their start and end apart: 2 -> 2, of which waited for: 1 -> 1; matrix products, arithmetic and copies ran while one was open for 1% -> 1% of each run, Pallas kernels for 0% -> 2%
where the time goes in v5:
time: 148 us; the launch traced here: 146 us
  blocking collectives  107 us (72%)
  starting transfers between devices  19.3 us (13%)
  Pallas kernels  11.1 us (8%)
  waiting for transfers between devices  4.35 us (3%)
  local copies, waits for them, and re-layouts  2.74 us (2%)
    unnamed x1, blocking collectives  107 us
    all_to_all x1, starting transfers between devices, per_device(): ends = lax.all_to_all(end_state, 'ctx', split_axis=0, concat_axis=0)  16.7 us
    pallas_call x1, Pallas kernels, per_device(): pl.pallas_call(product_kernel, out_shape=shape((groups * block, width)),...  6.24 us
    all_to_all x1, waiting for transfers between devices, per_device(): ends = lax.all_to_all(end_state, 'ctx', split_axis=0, concat_axis=0)  4.34 us
  transfers between devices with their start and end apart: 2, of which 1 were waited for; matrix products, arithmetic and copies ran while one was open for 1% of the time, Pallas kernels for 2%

profile of v5, /device:TPU:6, one launch (start us, length us, event | category | flops | bytes accessed | tf_op | source)
XLA Modules:
  0.0 146.0 jit_solution(7600644567026486486)
XLA Ops:
  0.0 2.1 %shard_map.73 = (f32[128,128]{1,0:T(8,128)}, f32[32,16,128]{2,1,0:T(8,128)}) custom-call(bf16[512,128]{1,0:T(8,128)(2,1)} %key_ref.3, bf16[512,128]{1,0:T(8,128)(2,1)} %value_ref.3, f32[16,128]{1,0:T(8,128)} %rate_ref.5), custom_call_target="tpu_custom_call" | custom-call | tf_op jit(solution)/shard_map/pallas_call | solution.py:163
  2.2 16.7 %all-to-all-start = ((f32[32,16,128]{2,1,0:T(8,128)}), f32[32,16,128]{2,1,0:T(8,128)S(1)}, u32[]{:S(2)}, u32[]{:S(2)}) async-start(f32[32,16,128]{2,1,0:T(8,128)} %get-tuple-element.9), calls=%async_computation | async-start | bytes 524288 | tf_op jit(solution)/shard_map/all_to_all | solution.py:168
  18.8 2.7 %shard_map.74 = (f32[512,128]{1,0:T(8,128)}, f32[16,128]{1,0:T(8,128)}) custom-call(f32[128,128]{1,0:T(8,128)} %get-tuple-element.10.chunk_ref, f32[16,128]{1,0:T(8,128)} %rate_ref.5, f32[16,128]{1,0:T(8,128)} %residue_ref.1, f32[1,128]{1,0:T(1,128)} %bitcast.5, bf16[512,128]{1,0:T(8,128)(2,1)} %query_ref.3, bf16[512,128]{1,0:T(8,128)(2,1)} %key_ref.3, ...), custom_call_target="tpu_custom_call" | custom-call | flops 4587520 | bytes 655360 | tf_op jit(solution)/shard_map/pallas_call | solution.py:169
  21.6 4.3 %all-to-all-done.ends_ref = f32[32,16,128]{2,1,0:T(8,128)S(1)} async-done(((f32[32,16,128]{2,1,0:T(8,128)}), f32[32,16,128]{2,1,0:T(8,128)S(1)}, u32[]{:S(2)}, u32[]{:S(2)}) %all-to-all-start) | async-done | bytes 262176 | tf_op jit(solution)/shard_map/all_to_all | solution.py:168
  25.9 0.0 copy-start
  25.9 0.7 copy-done
  26.6 6.2 %shard_map.75 = f32[16864,128]{1,0:T(8,128)} custom-call(s32[1]{0:T(128)} %bitcast.index_ref, f32[32,16,128]{2,1,0:T(8,128)} %copy-done, f32[16,128]{1,0:T(8,128)} %rate_ref.5, f32[16,128]{1,0:T(8,128)} %get-tuple-element.11.weight_ref, bf16[512,128]{1,0:T(8,128)(2,1)} %query_ref.3, f32[512,128]{1,0:T(8,128)} %get-tuple-element.12.local_ref, ...), custom_call_target="tpu_custom_call" | custom-call | tf_op jit(solution)/shard_map/pallas_call | solution.py:175
  32.9 107.1 %fusion = f32[528,128]{1,0:T(8,128)S(1)} fusion(f32[16864,128]{1,0:T(8,128)} %shard_map.75), kind=kCustom, calls=%all-reduce-scatter | all-reduce-scatter fusion | flops 2162689 | bytes 8908800
  140.0 2.7 %collective-permute-start = (f32[31,128]{1,0:T(8,128)S(1)}, f32[31,128]{1,0:T(8,128)S(1)}, u32[]{:S(2)}, u32[]{:S(2)}) collective-permute-start(f32[31,128]{1,0:T(8,128)S(1)} %slice.5), channel_id=1, source_target_pairs={{0,1},{1,2},{2,3},{3,4},{4,5},{5,6},{6,7},{7,8},{8,9},{9,10},{10,1... | collective-permute-start | bytes 47624
  142.7 1.3 dynamic-slice.4
  144.6 0.0 collective-permute-done
  144.6 0.7 concatenate
  145.4 0.7 fusion.1
  (2 shorter events, 0.0 us)
Async XLA Ops:
  2.2 23.8 %all-to-all-start = ((f32[32,16,128]{2,1,0:T(8,128)}), f32[32,16,128]{2,1,0:T(8,128)S(1)}, u32[]{:S(2)}, u32[]{:S(2)}) async-start(f32[32,16,128]{2,1,0:T(8,128)} %get-tuple-element.9), calls=%async_computation | async-start | bytes 524288 | tf_op jit(solution)/shard_map/all_to_all | solution.py:168
  25.9 0.7 copy-start
  140.0 4.6 %collective-permute-start = (f32[31,128]{1,0:T(8,128)S(1)}, f32[31,128]{1,0:T(8,128)S(1)}, u32[]{:S(2)}, u32[]{:S(2)}) collective-permute-start(f32[31,128]{1,0:T(8,128)S(1)} %slice.5), channel_id=1, source_target_pairs={{0,1},{1,2},{2,3},{3,4},{4,5},{5,6},{6,7},{7,8},{8,9},{9,10},{10,1... | collective-permute-start | bytes 47624

commit v6 on v5

--- a/solution.py
+++ b/solution.py
@@ -88,18 +88,14 @@
     weight_ref,
     query_ref,
     local_ref,
-    out_weight_hbm,
+    out_weight_ref,
     product_hbm,
     start_ref,
     conv_ref,
     shifted_ref,
-    out_weight_ref,
     product_ref,
-    load_sem,
     store_sems,
 ):
-    load = pltpu.make_async_copy(out_weight_hbm, out_weight_ref, load_sem)
-    load.start()
     modes = rate_ref.shape[0]
     length, width = query_ref.shape
     steps = length // chunks
@@ -125,7 +121,6 @@
     lax.fori_loop(0, steps, step, tails, unroll=4)
     conv_ref[...] = ((0.5 * query_ref[...].astype(jnp.float32)) * conv_ref[...]).astype(jnp.bfloat16).astype(jnp.float32)
 
-    load.wait()
     stores = []
     groups = out_weight_ref.shape[1] // width
     block = product_ref.shape[0] // groups
@@ -175,15 +170,13 @@
     product = pl.pallas_call(
         product_kernel,
         out_shape=shape((groups * block, width)),
-        in_specs=[pl.BlockSpec(memory_space=pltpu.SMEM)] + [vmem] * 5 + [pl.BlockSpec(memory_space=pl.ANY)],
+        in_specs=[pl.BlockSpec(memory_space=pltpu.SMEM)] + [vmem] * 6,
         out_specs=pl.BlockSpec(memory_space=pl.ANY),
         scratch_shapes=[
             pltpu.VMEM((chunks * modes, width), jnp.float32),
             pltpu.VMEM((length, width), jnp.float32),
             pltpu.VMEM((length + 16, width), jnp.float32),
-            pltpu.VMEM(out_weight.shape, jnp.bfloat16),
             pltpu.VMEM((groups * block, width), jnp.float32),
-            pltpu.SemaphoreType.DMA,
             pltpu.SemaphoreType.DMA((groups,)),
         ],
         compiler_params=pltpu.CompilerParams(vmem_limit_bytes=60 * 1024 * 1024),

time: 148 us -> 147 us (level)
  no operation moved by 1% of the time
where the time goes in v6:
time: 147 us; the launch traced here: 146 us
  blocking collectives  107 us (73%)
  starting transfers between devices  19.3 us (13%)
  Pallas kernels  10.8 us (7%)
  waiting for transfers between devices  4.35 us (3%)
  local copies, waits for them, and re-layouts  2.74 us (2%)
    unnamed x1, blocking collectives  107 us
    all_to_all x1, starting transfers between devices, per_device(): ends = lax.all_to_all(end_state, 'ctx', split_axis=0, concat_axis=0)  16.7 us
    pallas_call x1, Pallas kernels, per_device(): pl.pallas_call(product_kernel, out_shape=shape((groups * block, width)),...  5.92 us
    all_to_all x1, waiting for transfers between devices, per_device(): ends = lax.all_to_all(end_state, 'ctx', split_axis=0, concat_axis=0)  4.34 us
  transfers between devices with their start and end apart: 2, of which 1 were waited for; matrix products, arithmetic and copies ran while one was open for 1% of the time, Pallas kernels for 2%

profile of v6, /device:TPU:6, one launch (start us, length us, event | category | flops | bytes accessed | tf_op | source)
XLA Modules:
  0.0 145.7 jit_solution(13042391081627263286)
XLA Ops:
  0.0 2.1 %shard_map.73 = (f32[128,128]{1,0:T(8,128)}, f32[32,16,128]{2,1,0:T(8,128)}) custom-call(bf16[512,128]{1,0:T(8,128)(2,1)} %key_ref.3, bf16[512,128]{1,0:T(8,128)(2,1)} %value_ref.3, f32[16,128]{1,0:T(8,128)} %rate_ref.5), custom_call_target="tpu_custom_call" | custom-call | tf_op jit(solution)/shard_map/pallas_call | solution.py:158
  2.2 16.7 %all-to-all-start = ((f32[32,16,128]{2,1,0:T(8,128)}), f32[32,16,128]{2,1,0:T(8,128)S(1)}, u32[]{:S(2)}, u32[]{:S(2)}) async-start(f32[32,16,128]{2,1,0:T(8,128)} %get-tuple-element.9), calls=%async_computation | async-start | bytes 524288 | tf_op jit(solution)/shard_map/all_to_all | solution.py:163
  18.8 2.7 %shard_map.74 = (f32[512,128]{1,0:T(8,128)}, f32[16,128]{1,0:T(8,128)}) custom-call(f32[128,128]{1,0:T(8,128)} %get-tuple-element.10.chunk_ref, f32[16,128]{1,0:T(8,128)} %rate_ref.5, f32[16,128]{1,0:T(8,128)} %residue_ref.1, f32[1,128]{1,0:T(1,128)} %bitcast.5, bf16[512,128]{1,0:T(8,128)(2,1)} %query_ref.3, bf16[512,128]{1,0:T(8,128)(2,1)} %key_ref.3, ...), custom_call_target="tpu_custom_call" | custom-call | flops 4587520 | bytes 655360 | tf_op jit(solution)/shard_map/pallas_call | solution.py:164
  21.6 4.3 %all-to-all-done.ends_ref = f32[32,16,128]{2,1,0:T(8,128)S(1)} async-done(((f32[32,16,128]{2,1,0:T(8,128)}), f32[32,16,128]{2,1,0:T(8,128)S(1)}, u32[]{:S(2)}, u32[]{:S(2)}) %all-to-all-start) | async-done | bytes 262176 | tf_op jit(solution)/shard_map/all_to_all | solution.py:163
  25.9 0.0 copy-start
  25.9 0.7 copy-done
  26.6 5.9 %shard_map.75 = f32[16864,128]{1,0:T(8,128)} custom-call(s32[1]{0:T(128)} %bitcast.index_ref, f32[32,16,128]{2,1,0:T(8,128)} %copy-done, f32[16,128]{1,0:T(8,128)} %rate_ref.5, f32[16,128]{1,0:T(8,128)} %get-tuple-element.11.weight_ref, bf16[512,128]{1,0:T(8,128)(2,1)} %query_ref.3, f32[512,128]{1,0:T(8,128)} %get-tuple-element.12.local_ref, ...), custom_call_target="tpu_custom_call" | custom-call | tf_op jit(solution)/shard_map/pallas_call | solution.py:170
  32.6 107.1 %fusion = f32[528,128]{1,0:T(8,128)S(1)} fusion(f32[16864,128]{1,0:T(8,128)} %shard_map.75), kind=kCustom, calls=%all-reduce-scatter | all-reduce-scatter fusion | flops 2162689 | bytes 8908800
  139.7 2.7 %collective-permute-start = (f32[31,128]{1,0:T(8,128)S(1)}, f32[31,128]{1,0:T(8,128)S(1)}, u32[]{:S(2)}, u32[]{:S(2)}) collective-permute-start(f32[31,128]{1,0:T(8,128)S(1)} %slice.5), channel_id=1, source_target_pairs={{0,1},{1,2},{2,3},{3,4},{4,5},{5,6},{6,7},{7,8},{8,9},{9,10},{10,1... | collective-permute-start | bytes 47624
  142.3 1.3 dynamic-slice.4
  144.3 0.0 collective-permute-done
  144.3 0.7 concatenate
  145.0 0.7 fusion.1
  (2 shorter events, 0.0 us)
Async XLA Ops:
  2.2 23.8 %all-to-all-start = ((f32[32,16,128]{2,1,0:T(8,128)}), f32[32,16,128]{2,1,0:T(8,128)S(1)}, u32[]{:S(2)}, u32[]{:S(2)}) async-start(f32[32,16,128]{2,1,0:T(8,128)} %get-tuple-element.9), calls=%async_computation | async-start | bytes 524288 | tf_op jit(solution)/shard_map/all_to_all | solution.py:163
  25.9 0.7 copy-start
  139.7 4.6 %collective-permute-start = (f32[31,128]{1,0:T(8,128)S(1)}, f32[31,128]{1,0:T(8,128)S(1)}, u32[]{:S(2)}, u32[]{:S(2)}) collective-permute-start(f32[31,128]{1,0:T(8,128)S(1)} %slice.5), channel_id=1, source_target_pairs={{0,1},{1,2},{2,3},{3,4},{4,5},{5,6},{6,7},{7,8},{8,9},{9,10},{10,1... | collective-permute-start | bytes 47624

commit v7 on v6

--- a/solution.py
+++ b/solution.py
@@ -124,21 +124,26 @@
     stores = []
     groups = out_weight_ref.shape[1] // width
     block = product_ref.shape[0] // groups
-    shifted_ref[...] = jnp.zeros_like(shifted_ref)
+    half = length // 2
     for first in range(8):
         shift = first * block % 8
-        shifted_ref[0:8, :] = jnp.zeros((8, width), jnp.float32)
-        shifted_ref[shift : shift + length, :] = conv_ref[...]
-        shifted_ref[length + shift : length + 16, :] = jnp.zeros((16 - shift, width), jnp.float32)
-        left = shifted_ref[...].astype(jnp.bfloat16)
+        lefts = []
+        for part in range(2):
+            shifted_ref[0:8, :] = jnp.zeros((8, width), jnp.float32)
+            shifted_ref[shift : shift + half, :] = conv_ref[part * half : (part + 1) * half, :]
+            shifted_ref[half + shift : half + 16, :] = jnp.zeros((16 - shift, width), jnp.float32)
+            lefts.append(shifted_ref[...].astype(jnp.bfloat16))
         members = range(first, groups, 8)
         for pair in zip(members[::2], members[1::2]):
             right = jnp.concatenate([out_weight_ref[:, g * width : (g + 1) * width] for g in pair], axis=1)
-            both = jnp.dot(left, right, preferred_element_type=jnp.float32)
+            both = [jnp.dot(left, right, preferred_element_type=jnp.float32) for left in lefts]
             for place, g in enumerate(pair):
                 base = g * block - shift
                 rows = (g + 1) * block - (first + 1) * block % 8 - base
-                product_ref[base : base + rows, :] = both[:rows, place * width : (place + 1) * width]
+                for part in range(2):
+                    product_ref[base : base + rows, part * width : (part + 1) * width] = both[part][
+                        :rows, place * width : (place + 1) * width
+                    ]
                 store = pltpu.make_async_copy(
                     product_ref.at[pl.ds(base, rows), :], product_hbm.at[pl.ds(base, rows), :], store_sems.at[g]
                 )
@@ -152,7 +157,8 @@
     length, width = query.shape
     modes = decay_rates.shape[0]
     groups = out_weight.shape[1] // width
-    block = length + 15
+    half = length // 2
+    block = half + 7
     shape = functools.partial(jax.ShapeDtypeStruct, dtype=jnp.float32)
     vmem = pl.BlockSpec(memory_space=pltpu.VMEM)
     chunk_states, end_state = pl.pallas_call(
@@ -169,20 +175,21 @@
     )(chunk_states, decay_rates, residues, skip_gain[None, :], query, key_proj, value)
     product = pl.pallas_call(
         product_kernel,
-        out_shape=shape((groups * block, width)),
+        out_shape=shape((groups * block, 2 * width)),
         in_specs=[pl.BlockSpec(memory_space=pltpu.SMEM)] + [vmem] * 6,
         out_specs=pl.BlockSpec(memory_space=pl.ANY),
         scratch_shapes=[
             pltpu.VMEM((chunks * modes, width), jnp.float32),
             pltpu.VMEM((length, width), jnp.float32),
-            pltpu.VMEM((length + 16, width), jnp.float32),
-            pltpu.VMEM((groups * block, width), jnp.float32),
+            pltpu.VMEM((half + 16, width), jnp.float32),
+            pltpu.VMEM((groups * block, 2 * width), jnp.float32),
             pltpu.SemaphoreType.DMA((groups,)),
         ],
         compiler_params=pltpu.CompilerParams(vmem_limit_bytes=60 * 1024 * 1024),
     )(lax.axis_index("ctx").reshape(1), ends, decay_rates, weights, query, local, out_weight)
     summed = lax.optimization_barrier(lax.psum_scatter(product, "tp", scatter_dimension=0, tiled=True))
-    return (2.0 * summed[:length]).astype(jnp.bfloat16)
+    joined = jnp.concatenate([summed[:half, :width], summed[:half, width:]])
+    return (2.0 * joined).astype(jnp.bfloat16)
 
 
 def solution(mesh):

time: 147 us -> 147 us (level)
  no operation moved by 1% of the time
where the time goes in v7:
time: 147 us; the launch traced here: 145 us
  blocking collectives  107 us (73%)
  starting transfers between devices  19.5 us (13%)
  Pallas kernels  10.8 us (7%)
  waiting for transfers between devices  4.35 us (3%)
  local copies, waits for them, and re-layouts  2.39 us (2%)
    unnamed x1, blocking collectives  107 us
    all_to_all x1, starting transfers between devices, per_device(): ends = lax.all_to_all(end_state, 'ctx', split_axis=0, concat_axis=0)  16.7 us
    pallas_call x1, Pallas kernels, per_device(): pl.pallas_call(product_kernel, out_shape=shape((groups * block, 2 * width...  5.86 us
    all_to_all x1, waiting for transfers between devices, per_device(): ends = lax.all_to_all(end_state, 'ctx', split_axis=0, concat_axis=0)  4.34 us
  transfers between devices with their start and end apart: 2, of which 1 were waited for; matrix products, arithmetic and copies ran while one was open for 1% of the time, Pallas kernels for 2%

profile of v7, /device:TPU:6, one launch (start us, length us, event | category | flops | bytes accessed | tf_op | source)
XLA Modules:
  0.0 145.5 jit_solution(6573722848551345782)
XLA Ops:
  0.0 2.2 %shard_map.73 = (f32[128,128]{1,0:T(8,128)}, f32[32,16,128]{2,1,0:T(8,128)}) custom-call(bf16[512,128]{1,0:T(8,128)(2,1)} %key_ref.3, bf16[512,128]{1,0:T(8,128)(2,1)} %value_ref.3, f32[16,128]{1,0:T(8,128)} %rate_ref.5), custom_call_target="tpu_custom_call" | custom-call | tf_op jit(solution)/shard_map/pallas_call | solution.py:164
  2.2 16.7 %all-to-all-start = ((f32[32,16,128]{2,1,0:T(8,128)}), f32[32,16,128]{2,1,0:T(8,128)S(1)}, u32[]{:S(2)}, u32[]{:S(2)}) async-start(f32[32,16,128]{2,1,0:T(8,128)} %get-tuple-element.9), calls=%async_computation | async-start | bytes 524288 | tf_op jit(solution)/shard_map/all_to_all | solution.py:169
  18.8 2.7 %shard_map.74 = (f32[512,128]{1,0:T(8,128)}, f32[16,128]{1,0:T(8,128)}) custom-call(f32[128,128]{1,0:T(8,128)} %get-tuple-element.10.chunk_ref, f32[16,128]{1,0:T(8,128)} %rate_ref.5, f32[16,128]{1,0:T(8,128)} %residue_ref.1, f32[1,128]{1,0:T(1,128)} %bitcast.5, bf16[512,128]{1,0:T(8,128)(2,1)} %query_ref.3, bf16[512,128]{1,0:T(8,128)(2,1)} %key_ref.3, ...), custom_call_target="tpu_custom_call" | custom-call | flops 4587520 | bytes 655360 | tf_op jit(solution)/shard_map/pallas_call | solution.py:170
  21.6 4.3 %all-to-all-done.ends_ref = f32[32,16,128]{2,1,0:T(8,128)S(1)} async-done(((f32[32,16,128]{2,1,0:T(8,128)}), f32[32,16,128]{2,1,0:T(8,128)S(1)}, u32[]{:S(2)}, u32[]{:S(2)}) %all-to-all-start) | async-done | bytes 262176 | tf_op jit(solution)/shard_map/all_to_all | solution.py:169
  25.9 0.0 copy-start
  25.9 0.7 copy-done
  26.6 5.9 %shard_map.75 = f32[8416,256]{1,0:T(8,128)} custom-call(s32[1]{0:T(128)} %bitcast.index_ref, f32[32,16,128]{2,1,0:T(8,128)} %copy-done, f32[16,128]{1,0:T(8,128)} %rate_ref.5, f32[16,128]{1,0:T(8,128)} %get-tuple-element.11.weight_ref, bf16[512,128]{1,0:T(8,128)(2,1)} %query_ref.3, f32[512,128]{1,0:T(8,128)} %get-tuple-element.12.local_ref, ...), custom_call_target="tpu_custom_call" | custom-call | tf_op jit(solution)/shard_map/pallas_call | solution.py:176
  32.5 107.1 %fusion = f32[264,256]{1,0:T(8,128)S(1)} fusion(f32[8416,256]{1,0:T(8,128)} %shard_map.75), kind=kCustom, calls=%all-reduce-scatter | all-reduce-scatter fusion | flops 2162689 | bytes 8892416
  139.6 2.8 %collective-permute-start = (f32[31,256]{1,0:T(8,128)S(1)}, f32[31,256]{1,0:T(8,128)S(1)}, u32[]{:S(2)}, u32[]{:S(2)}) collective-permute-start(f32[31,256]{1,0:T(8,128)S(1)} %slice.10), channel_id=1, source_target_pairs={{0,1},{1,2},{2,3},{3,4},{4,5},{5,6},{6,7},{7,8},{8,9},{9,10},{10,1... | collective-permute-start | bytes 95240
  142.5 1.3 dynamic-slice.4
  144.4 0.0 collective-permute-done
  144.4 0.3 concatenate.4
  144.8 0.7 fusion.1
  (3 shorter events, 0.1 us)
Async XLA Ops:
  2.2 23.8 %all-to-all-start = ((f32[32,16,128]{2,1,0:T(8,128)}), f32[32,16,128]{2,1,0:T(8,128)S(1)}, u32[]{:S(2)}, u32[]{:S(2)}) async-start(f32[32,16,128]{2,1,0:T(8,128)} %get-tuple-element.9), calls=%async_computation | async-start | bytes 524288 | tf_op jit(solution)/shard_map/all_to_all | solution.py:169
  25.9 0.7 copy-start
  139.6 4.8 %collective-permute-start = (f32[31,256]{1,0:T(8,128)S(1)}, f32[31,256]{1,0:T(8,128)S(1)}, u32[]{:S(2)}, u32[]{:S(2)}) collective-permute-start(f32[31,256]{1,0:T(8,128)S(1)} %slice.10), channel_id=1, source_target_pairs={{0,1},{1,2},{2,3},{3,4},{4,5},{5,6},{6,7},{7,8},{8,9},{9,10},{10,1... | collective-permute-start | bytes 95240
